TPU v7x, 256 devices: a whole 4x4x8 slice. The times are simulated.
256 devices in a mesh: prow: 8 (over x, core), pcol: 32 (over z, y).
Axes of the slice: x: 4, y: 4, z: 8, core: 2. Of those that a mesh axis runs over, the one named last changes fastest.
Arguments:
- rhs: float32 [64, 65536], P(None, 'pcol'), may hold values from -6 to 6
- pivots: int32 [65536], P('pcol'), may hold values from 0 to 65535, as said below
- tile_of: int32 [256], replicated, may hold values from 0 to 255, as said below
- upper_rows: bfloat16 [3, 2048, 65536], P(None, 'prow', 'pcol'), may hold values from -0.125 to 0.125
- upper_inv: bfloat16 [3, 2048, 2048], P(None, 'pcol', 'prow'), may hold values from -0.125 to 0.125
- lower_rows: bfloat16 [3, 2048, 65536], P(None, 'prow', 'pcol'), may hold values from -0.125 to 0.125
- lower_inv: bfloat16 [3, 2048, 2048], P(None, 'prow', 'pcol'), may hold values from -0.125 to 0.125
- solved: float32 [64, 65536], P(None, 'pcol'), may hold values from -6 to 6
Outputs:
- forward: float32 [64, 65536], P(None, 'pcol')
- backward: float32 [64, 65536], P(None, 'pcol')
Inputs may be any that keep to these rules, and one draw needn't show every extreme that they name: pivots[p] lies in the same tile of 256 storage columns as p, and each column of a tile appears once. `tile_of`: storage tile d * 256 / 32 + l holds global tile l * 32 + c(d), c a permutation of the process columns.
All inputs are finite; a program needn't handle non-finite values.
Results may differ from a plain program's by a relative error of at most 0.015.
Values may be sent and summed in bfloat16 or wider, within the bound.
No kernel may reach another device: no remote copies, remote signals or barrier semaphores. Data moves between devices by JAX's collectives and lax.ppermute only.
A program may use at most 64 MiB of HBM per device.

v0:
```python
import jax
import jax.numpy as jnp
from jax import lax
from jax.sharding import PartitionSpec as P

NB = 2048
TILE = 256
STEPS = 3


def body(rhs, pivots, tile_of, upper_rows, upper_inv, lower_rows, lower_inv, solved):
    pcol_index = lax.axis_index("pcol")
    prow_index = lax.axis_index("prow")
    width_here = rhs.shape[1]
    tiles_here = width_here // TILE
    tiles_block = NB // TILE
    prow_rows = upper_rows.shape[1]
    count = rhs.shape[0]
    my_tiles = lax.dynamic_slice_in_dim(tile_of, pcol_index * tiles_here, tiles_here)
    my_blocks = my_tiles // tiles_block
    cell_blocks = jnp.repeat(my_blocks, TILE)

    def locate(step):
        match = my_blocks == step
        holds = jnp.any(match)
        tile_slot = jnp.argmax(match)
        block_place = my_tiles[tile_slot] % tiles_block
        return (holds, tile_slot, block_place)

    def write_block(field, block_full, step):
        holds, tile_slot, block_place = locate(step)
        piece = lax.dynamic_slice_in_dim(block_full, block_place * TILE, TILE, 1).astype(
            jnp.float32
        )
        written = lax.dynamic_update_slice_in_dim(field, piece, tile_slot * TILE, 1)
        return jnp.where(holds, written, field)

    state = jnp.take(rhs, pivots - pcol_index * width_here, axis=1)
    finished = []
    for step in range(STEPS):
        holds, tile_slot, block_place = locate(step)
        piece = lax.dynamic_slice_in_dim(state, tile_slot * TILE, TILE, 1)
        piece = jnp.where(holds, piece, 0.0)
        buffer = jnp.zeros((count, NB), jnp.float32)
        buffer = lax.dynamic_update_slice_in_dim(buffer, piece, block_place * TILE, 1)
        block_part = lax.psum_scatter(
            buffer.astype(jnp.bfloat16), "pcol", scatter_dimension=1, tiled=True
        )
        inverse_part = jnp.dot(block_part, upper_inv[step], preferred_element_type=jnp.float32)
        block_rows = lax.psum(inverse_part, "pcol").astype(jnp.bfloat16)
        block_full = lax.all_gather(block_rows, "prow", axis=1, tiled=True)
        update = jnp.dot(block_rows, upper_rows[step], preferred_element_type=jnp.float32)
        total = lax.psum(update, "prow")
        state = state - jnp.where(cell_blocks > step, total, 0.0)
        state = write_block(state, block_full, step)
        finished.append(block_full)
    solution = solved
    for step in reversed(range(STEPS)):
        known = jnp.where(cell_blocks > step, solution, 0.0).astype(jnp.bfloat16)
        partial_value = lax.dot_general(
            known, lower_rows[step], (((1,), (1,)), ((), ())), preferred_element_type=jnp.float32
        )
        sums = lax.psum(partial_value, "pcol")
        own_rows = lax.dynamic_slice_in_dim(
            finished[step], prow_index * prow_rows, prow_rows, 1
        ).astype(jnp.float32)
        resid = (own_rows - sums).astype(jnp.bfloat16)
        inverse_part = jnp.dot(resid, lower_inv[step], preferred_element_type=jnp.float32)
        new_cols = lax.psum(inverse_part, "prow").astype(jnp.bfloat16)
        new_block = lax.all_gather(new_cols, "pcol", axis=1, tiled=True)
        solution = write_block(solution, new_block, step)
    return (state, solution)


def solution(mesh):
    return jax.shard_map(
        body,
        mesh=mesh,
        in_specs=(
            P(None, "pcol"),
            P("pcol"),
            P(),
            P(None, "prow", "pcol"),
            P(None, "pcol", "prow"),
            P(None, "prow", "pcol"),
            P(None, "prow", "pcol"),
            P(None, "pcol"),
        ),
        out_specs=(P(None, "pcol"), P(None, "pcol")),
        check_vma=False,
    )
```

profile of v0, /device:TPU:8, one launch (start us, length us, event | category | flops | bytes accessed | tf_op | source)
XLA Modules:
  0.0 1755.8 jit_solution(12627563569382211011)
XLA Ops:
  24.7 5.5 gather_fusion
  32.3 215.0 %reduce-scatter.10.cloned.1.call-done = bf16[64,64]{1,0:T(8,128)(2,1)} async-done(((bf16[2048,64]{1,0:T(8,128)(2,1)}), bf16[64,64]{1,0:T(8,128)(2,1)}) %reduce-scatter.10.cloned.1.call-update) | async-done | bytes 8208
  248.2 136.2 %psum.84 = bf16[64,256]{1,0:T(8,128)(2,1)S(1)} all-reduce(f32[64,256]{1,0:T(8,128)S(1)} %fusion.34), channel_id=1, replica_groups=mesh['prow'=8,'pcol'=32] {'pcol'}, use_global_device_ids=true, to_apply=%region_3.4 | all-reduce | flops 16384 | bytes 98304 | tf_op jit(solution)/shard_map/psum | solution.py:50
  384.4 2.3 fusion.10
  389.3 13.2 all_gather.18
  402.5 52.6 %all-reduce.7.cloned.1.call-done = f32[64,2048]{1,0:T(8,128)} async-done(((f32[64,2048]{1,0:T(8,128)}), f32[64,2048]{1,0:T(8,128)}) %all-reduce.7.cloned.1.call-update) | async-done | bytes 524304 | tf_op jit(solution)/shard_map/psum | solution.py:53
  458.7 212.1 %reduce-scatter.12.cloned.1.call-done = bf16[64,64]{1,0:T(8,128)(2,1)} async-done(((bf16[2048,64]{1,0:T(8,128)(2,1)}), bf16[64,64]{1,0:T(8,128)(2,1)}) %reduce-scatter.12.cloned.1.call-update) | async-done | bytes 8208
  671.7 136.1 %psum.86 = bf16[64,256]{1,0:T(8,128)(2,1)S(1)} all-reduce(f32[64,256]{1,0:T(8,128)S(1)} %fusion.32), channel_id=1, replica_groups=mesh['prow'=8,'pcol'=32] {'pcol'}, use_global_device_ids=true, to_apply=%region_8.9 | all-reduce | flops 16384 | bytes 98304 | tf_op jit(solution)/shard_map/psum | solution.py:50
  807.8 2.3 fusion.8
  812.6 13.1 all_gather.19
  825.8 52.8 %all-reduce.9.cloned.1.call-done = f32[64,2048]{1,0:T(8,128)} async-done(((f32[64,2048]{1,0:T(8,128)}), f32[64,2048]{1,0:T(8,128)}) %all-reduce.9.cloned.1.call-update) | async-done | bytes 524304 | tf_op jit(solution)/shard_map/psum | solution.py:53
  882.2 2.3 fusion.4
  884.6 209.7 %reduce-scatter.14.cloned.1.call-done = bf16[64,64]{1,0:T(8,128)(2,1)} async-done(((bf16[2048,64]{1,0:T(8,128)(2,1)}), bf16[64,64]{1,0:T(8,128)(2,1)}) %reduce-scatter.14.cloned.1.call-update) | async-done | bytes 8208
  1095.2 136.1 %psum.88 = bf16[64,256]{1,0:T(8,128)(2,1)S(1)} all-reduce(f32[64,256]{1,0:T(8,128)S(1)} %fusion.30), channel_id=1, replica_groups=mesh['prow'=8,'pcol'=32] {'pcol'}, use_global_device_ids=true, to_apply=%region_13.14 | all-reduce | flops 16384 | bytes 98304 | tf_op jit(solution)/shard_map/psum | solution.py:50
  1231.3 13.1 all_gather.20
  1245.4 25.8 %psum.91 = bf16[64,64]{1,0:T(8,128)(2,1)S(1)} all-reduce(f32[64,64]{1,0:T(8,128)S(1)} %fusion.24), channel_id=1, replica_groups=mesh['prow'=8,'pcol'=32] {'prow'}, use_global_device_ids=true, to_apply=%region_16.17 | all-reduce | flops 4096 | bytes 24576 | tf_op jit(solution)/shard_map/psum | solution.py:69
  1271.3 51.7 %all_gather.21 = bf16[64,2048]{0,1:T(8,128)(2,1)S(1)} all-gather(bf16[64,64]{0,1:T(8,128)(2,1)S(1)} %copy.14), channel_id=1, replica_groups=mesh['prow'=8,'pcol'=32] {'pcol'}, dimensions={1}, use_global_device_ids=true | all-gather | bytes 270336 | tf_op jit(solution)/shard_map/all_gather | solution.py:70
  1326.1 136.4 %all-reduce.15.cloned.1.call-done = f32[64,256]{1,0:T(8,128)} async-done(((f32[64,256]{1,0:T(8,128)}), f32[64,256]{1,0:T(8,128)}) %all-reduce.15.cloned.1.call-update) | async-done | bytes 65552 | tf_op jit(solution)/shard_map/psum | solution.py:63
  1463.4 23.6 %psum.93 = bf16[64,64]{1,0:T(8,128)(2,1)S(1)} all-reduce(f32[64,64]{1,0:T(8,128)S(1)} %fusion.25), channel_id=1, replica_groups=mesh['prow'=8,'pcol'=32] {'prow'}, use_global_device_ids=true, to_apply=%region_18.19 | all-reduce | flops 4096 | bytes 24576 | tf_op jit(solution)/shard_map/psum | solution.py:69
  1487.2 47.4 %all_gather.22 = bf16[64,2048]{0,1:T(8,128)(2,1)S(1)} all-gather(bf16[64,64]{0,1:T(8,128)(2,1)S(1)} %copy.16), channel_id=1, replica_groups=mesh['prow'=8,'pcol'=32] {'pcol'}, dimensions={1}, use_global_device_ids=true | all-gather | bytes 270336 | tf_op jit(solution)/shard_map/all_gather | solution.py:70
  1537.8 2.3 fusion.6
  1540.1 133.5 %all-reduce.17.cloned.1.call-done = f32[64,256]{1,0:T(8,128)} async-done(((f32[64,256]{1,0:T(8,128)}), f32[64,256]{1,0:T(8,128)}) %all-reduce.17.cloned.1.call-update) | async-done | bytes 65552 | tf_op jit(solution)/shard_map/psum | solution.py:63
  1674.6 23.6 %psum.95 = bf16[64,64]{1,0:T(8,128)(2,1)S(1)} all-reduce(f32[64,64]{1,0:T(8,128)S(1)} %fusion.26), channel_id=1, replica_groups=mesh['prow'=8,'pcol'=32] {'prow'}, use_global_device_ids=true, to_apply=%region_20.21 | all-reduce | flops 4096 | bytes 24576 | tf_op jit(solution)/shard_map/psum | solution.py:69
  1698.3 47.5 %all_gather.23 = bf16[64,2048]{0,1:T(8,128)(2,1)S(1)} all-gather(bf16[64,64]{0,1:T(8,128)(2,1)S(1)} %copy.18), channel_id=1, replica_groups=mesh['prow'=8,'pcol'=32] {'pcol'}, dimensions={1}, use_global_device_ids=true | all-gather | bytes 270336 | tf_op jit(solution)/shard_map/all_gather | solution.py:70
  (81 shorter events, 34.0 us)
Async XLA Ops:
  7.2 240.1 %reduce-scatter.10.cloned.1.call-start = ((), (), s32[]{:S(2)}) async-start(), calls=%async_computation.9 | async-start | bytes 540672
  30.1 217.2 %copy-start.2 = (bf16[3,64,256]{2,1,0:T(8,128)(2,1)S(1)}, bf16[3,64,256]{2,1,0:T(8,128)(2,1)}, u32[]{:S(2)}) copy-start(bf16[3,64,256]{2,1,0:T(8,128)(2,1)} %param.12) | copy-start | bytes 294916
  32.3 422.8 %all-reduce.7.cloned.1.call-start = ((), (), s32[]{:S(2)}) async-start(), calls=%async_computation.3 | async-start | bytes 1048576 | tf_op jit(solution)/shard_map/psum | solution.py:53
  386.7 284.1 %reduce-scatter.12.cloned.1.call-start = ((), (), s32[]{:S(2)}) async-start(), calls=%async_computation.10 | async-start | bytes 540672
  458.7 419.9 %all-reduce.9.cloned.1.call-start = ((), (), s32[]{:S(2)}) async-start(), calls=%async_computation.4 | async-start | bytes 1048576 | tf_op jit(solution)/shard_map/psum | solution.py:53
  810.1 434.4 %copy-start.3 = (bf16[3,256,64]{1,2,0:T(8,128)(2,1)S(1)}, bf16[3,256,64]{1,2,0:T(8,128)(2,1)}, u32[]{:S(2)}) copy-start(bf16[3,256,64]{1,2,0:T(8,128)(2,1)} %param.14) | copy-start | bytes 294916
  810.1 284.2 %reduce-scatter.14.cloned.1.call-start = ((), (), s32[]{:S(2)}) async-start(), calls=%async_computation.11 | async-start | bytes 540672
  882.0 362.4 %all-reduce.13.cloned.1.call-start = ((), (), s32[]{:S(2)}) async-start(), calls=%async_computation.6 | async-start | bytes 131072 | tf_op jit(solution)/shard_map/psum | solution.py:63
  884.5 578.0 %all-reduce.15.cloned.1.call-start = ((), (), s32[]{:S(2)}) async-start(), calls=%async_computation.7 | async-start | bytes 131072 | tf_op jit(solution)/shard_map/psum | solution.py:63
  1326.1 347.6 %all-reduce.17.cloned.1.call-start = ((), (), s32[]{:S(2)}) async-start(), calls=%async_computation.8 | async-start | bytes 131072 | tf_op jit(solution)/shard_map/psum | solution.py:63
  1537.7 208.9 %all-reduce.11.cloned.1.call-start = ((), (), s32[]{:S(2)}) async-start(), calls=%async_computation.5 | async-start | bytes 1048576 | tf_op jit(solution)/shard_map/psum | solution.py:53
  1746.6 1.9 copy-start
  1748.5 0.8 copy-start.1
Sparse Core Ops, SparseCore 0:
  32.4 214.8 reduce-scatter.9
  386.8 68.2 all-reduce.6
  459.5 211.2 reduce-scatter.11
  810.3 68.2 all-reduce.8
  882.8 211.4 reduce-scatter.13
  1098.6 138.1 all-reduce.12
  1326.2 136.2 all-reduce.14
  1537.8 135.7 all-reduce.16
  1676.7 64.1 all-reduce.10
where the time goes:
time: 1760 us
  waiting for transfers between devices  1010 us (57%)
  blocking collectives  667 us (38%)
  between operations  27.6 us (2%)
  matrix products  19.4 us (1%)
    unnamed x12, waiting for transfers between devices  637 us
    psum x3, blocking collectives, body(): block_rows = lax.psum(inverse_part, 'pcol').astype(jnp.bfloat16)  408 us
    psum x3, waiting for transfers between devices, body(): sums = lax.psum(partial_value, 'pcol')  270 us
    all_gather x3, blocking collectives, body(): new_block = lax.all_gather(new_cols, 'pcol', axis=1, tiled=True)  147 us
    psum x3, waiting for transfers between devices, body(): total = lax.psum(update, 'prow')  105 us
    psum x3, blocking collectives, body(): new_cols = lax.psum(inverse_part, 'prow').astype(jnp.bfloat16)  73 us
    all_gather x3, blocking collectives, body(): block_full = lax.all_gather(block_rows, 'prow', axis=1, tiled=True)  39.4 us
  transfers between devices with their start and end apart: 9, of which 7 were waited for; matrix products, arithmetic and copies ran while one was open for 0% of the time, Pallas kernels for 0%

commit v1 on v0

--- a/solution.py
+++ b/solution.py
@@ -60,7 +60,7 @@
         partial_value = lax.dot_general(
             known, lower_rows[step], (((1,), (1,)), ((), ())), preferred_element_type=jnp.float32
         )
-        sums = lax.psum(partial_value, "pcol")
+        sums = jnp.sum(lax.all_gather(partial_value, "pcol"), axis=0)
         own_rows = lax.dynamic_slice_in_dim(
             finished[step], prow_index * prow_rows, prow_rows, 1
         ).astype(jnp.float32)

time: 1760 us -> 1630 us (0.926)
  waiting for transfers between devices: 1010 us -> 885 us
    psum x3 -> x0, waiting for transfers between devices: 270 us -> none  [body(): sums = lax.psum(partial_value, 'pcol')]
    all_gather x0 -> x3, waiting for transfers between devices: none -> 143 us  [body(): sums = jnp.sum(lax.all_gather(partial_value, 'pcol'), axis=0)]
  transfers between devices with their start and end apart: 9 -> 9, of which waited for: 7 -> 7; matrix products, arithmetic and copies ran while one was open for 0% -> 1% of each run, Pallas kernels for 0% -> 0%
where the time goes in v1:
time: 1630 us
  waiting for transfers between devices  885 us (54%)
  blocking collectives  669 us (41%)
  between operations  27.6 us (2%)
  other arithmetic  19.6 us (1%)
  matrix products  16.9 us (1%)
    unnamed x12, waiting for transfers between devices  637 us
    psum x3, blocking collectives, body(): block_rows = lax.psum(inverse_part, 'pcol').astype(jnp.bfloat16)  409 us
    all_gather x3, blocking collectives, body(): new_block = lax.all_gather(new_cols, 'pcol', axis=1, tiled=True)  148 us
    all_gather x3, waiting for transfers between devices, body(): sums = jnp.sum(lax.all_gather(partial_value, 'pcol'), axis=0)  143 us
    psum x3, waiting for transfers between devices, body(): total = lax.psum(update, 'prow')  105 us
    psum x3, blocking collectives, body(): new_cols = lax.psum(inverse_part, 'prow').astype(jnp.bfloat16)  73 us
    all_gather x3, blocking collectives, body(): block_full = lax.all_gather(block_rows, 'prow', axis=1, tiled=True)  39.4 us
  transfers between devices with their start and end apart: 9, of which 7 were waited for; matrix products, arithmetic and copies ran while one was open for 1% of the time, Pallas kernels for 0%

profile of v1, /device:TPU:8, one launch (start us, length us, event | category | flops | bytes accessed | tf_op | source)
XLA Modules:
  0.0 1633.1 jit_solution(9475931321389946059)
XLA Ops:
  24.4 5.5 gather_fusion
  32.1 215.0 %reduce-scatter.10.cloned.1.call-done = bf16[64,64]{1,0:T(8,128)(2,1)} async-done(((bf16[2048,64]{1,0:T(8,128)(2,1)}), bf16[64,64]{1,0:T(8,128)(2,1)}) %reduce-scatter.10.cloned.1.call-update) | async-done | bytes 8208
  248.0 136.2 %psum.63 = bf16[64,256]{1,0:T(8,128)(2,1)S(1)} all-reduce(f32[64,256]{1,0:T(8,128)S(1)} %fusion.34), channel_id=1, replica_groups=mesh['prow'=8,'pcol'=32] {'pcol'}, use_global_device_ids=true, to_apply=%region_3.4 | all-reduce | flops 16384 | bytes 98304 | tf_op jit(solution)/shard_map/psum | solution.py:50
  384.1 2.3 fusion.10
  389.2 13.2 all_gather.36
  402.4 52.5 %all-reduce.4.cloned.1.call-done = f32[64,2048]{1,0:T(8,128)} async-done(((f32[64,2048]{1,0:T(8,128)}), f32[64,2048]{1,0:T(8,128)}) %all-reduce.4.cloned.1.call-update) | async-done | bytes 524304 | tf_op jit(solution)/shard_map/psum | solution.py:53
  458.4 212.2 %reduce-scatter.12.cloned.1.call-done = bf16[64,64]{1,0:T(8,128)(2,1)} async-done(((bf16[2048,64]{1,0:T(8,128)(2,1)}), bf16[64,64]{1,0:T(8,128)(2,1)}) %reduce-scatter.12.cloned.1.call-update) | async-done | bytes 8208
  671.5 136.1 %psum.65 = bf16[64,256]{1,0:T(8,128)(2,1)S(1)} all-reduce(f32[64,256]{1,0:T(8,128)S(1)} %fusion.32), channel_id=1, replica_groups=mesh['prow'=8,'pcol'=32] {'pcol'}, use_global_device_ids=true, to_apply=%region_8.9 | all-reduce | flops 16384 | bytes 98304 | tf_op jit(solution)/shard_map/psum | solution.py:50
  807.6 2.3 fusion.8
  812.6 13.1 all_gather.37
  825.7 52.6 %all-reduce.6.cloned.1.call-done = f32[64,2048]{1,0:T(8,128)} async-done(((f32[64,2048]{1,0:T(8,128)}), f32[64,2048]{1,0:T(8,128)}) %all-reduce.6.cloned.1.call-update) | async-done | bytes 524304 | tf_op jit(solution)/shard_map/psum | solution.py:53
  884.4 209.6 %reduce-scatter.14.cloned.1.call-done = bf16[64,64]{1,0:T(8,128)(2,1)} async-done(((bf16[2048,64]{1,0:T(8,128)(2,1)}), bf16[64,64]{1,0:T(8,128)(2,1)}) %reduce-scatter.14.cloned.1.call-update) | async-done | bytes 8208
  1095.0 136.5 %psum.67 = bf16[64,256]{1,0:T(8,128)(2,1)S(1)} all-reduce(f32[64,256]{1,0:T(8,128)S(1)} %fusion.30), channel_id=1, replica_groups=mesh['prow'=8,'pcol'=32] {'pcol'}, use_global_device_ids=true, to_apply=%region_13.14 | all-reduce | flops 16384 | bytes 98304 | tf_op jit(solution)/shard_map/psum | solution.py:50
  1231.4 13.1 all_gather.38
  1246.4 25.8 %psum.69 = bf16[64,64]{1,0:T(8,128)(2,1)S(1)} all-reduce(f32[64,64]{1,0:T(8,128)S(1)} %fusion.24), channel_id=1, replica_groups=mesh['prow'=8,'pcol'=32] {'prow'}, use_global_device_ids=true, to_apply=%region_16.17 | all-reduce | flops 4096 | bytes 24576 | tf_op jit(solution)/shard_map/psum | solution.py:69
  1272.3 51.7 %all_gather.41 = bf16[64,2048]{0,1:T(8,128)(2,1)S(1)} all-gather(bf16[64,64]{0,1:T(8,128)(2,1)S(1)} %copy.14), channel_id=1, replica_groups=mesh['prow'=8,'pcol'=32] {'pcol'}, dimensions={1}, use_global_device_ids=true | all-gather | bytes 270336 | tf_op jit(solution)/shard_map/all_gather | solution.py:70
  1324.8 2.3 fusion.2
  1327.2 2.3 fusion.6
  1329.6 71.6 %all-gather.9.cloned.1.call-done = f32[2048,256]{1,0:T(8,128)} async-done(((f32[64,256]{1,0:T(8,128)}), f32[2048,256]{1,0:T(8,128)}) %all-gather.9.cloned.1.call-update) | async-done | bytes 2097168 | tf_op jit(solution)/shard_map/all_gather | solution.py:63
  1403.0 23.6 %psum.70 = bf16[64,64]{1,0:T(8,128)(2,1)S(1)} all-reduce(f32[64,64]{1,0:T(8,128)S(1)} %fusion.25), channel_id=1, replica_groups=mesh['prow'=8,'pcol'=32] {'prow'}, use_global_device_ids=true, to_apply=%region_18.19 | all-reduce | flops 4096 | bytes 24576 | tf_op jit(solution)/shard_map/psum | solution.py:69
  1426.7 48.1 %all_gather.44 = bf16[64,2048]{0,1:T(8,128)(2,1)S(1)} all-gather(bf16[64,64]{0,1:T(8,128)(2,1)S(1)} %copy.16), channel_id=1, replica_groups=mesh['prow'=8,'pcol'=32] {'pcol'}, dimensions={1}, use_global_device_ids=true | all-gather | bytes 270336 | tf_op jit(solution)/shard_map/all_gather | solution.py:70
  1479.7 71.7 %all-gather.11.cloned.1.call-done = f32[2048,256]{1,0:T(8,128)} async-done(((f32[64,256]{1,0:T(8,128)}), f32[2048,256]{1,0:T(8,128)}) %all-gather.11.cloned.1.call-update) | async-done | bytes 2097168 | tf_op jit(solution)/shard_map/all_gather | solution.py:63
  1553.3 23.6 %psum.71 = bf16[64,64]{1,0:T(8,128)(2,1)S(1)} all-reduce(f32[64,64]{1,0:T(8,128)S(1)} %fusion.26), channel_id=1, replica_groups=mesh['prow'=8,'pcol'=32] {'prow'}, use_global_device_ids=true, to_apply=%region_20.21 | all-reduce | flops 4096 | bytes 24576 | tf_op jit(solution)/shard_map/psum | solution.py:69
  1577.0 48.0 %all_gather.47 = bf16[64,2048]{0,1:T(8,128)(2,1)S(1)} all-gather(bf16[64,64]{0,1:T(8,128)(2,1)S(1)} %copy.18), channel_id=1, replica_groups=mesh['prow'=8,'pcol'=32] {'pcol'}, dimensions={1}, use_global_device_ids=true | all-gather | bytes 270336 | tf_op jit(solution)/shard_map/all_gather | solution.py:70
  (84 shorter events, 36.7 us)
Async XLA Ops:
  7.2 239.9 %reduce-scatter.10.cloned.1.call-start = ((), (), s32[]{:S(2)}) async-start(), calls=%async_computation.9 | async-start | bytes 540672
  29.9 217.2 %copy-start.2 = (bf16[3,64,256]{2,1,0:T(8,128)(2,1)S(1)}, bf16[3,64,256]{2,1,0:T(8,128)(2,1)}, u32[]{:S(2)}) copy-start(bf16[3,64,256]{2,1,0:T(8,128)(2,1)} %param.12) | copy-start | bytes 294916
  32.0 422.8 %all-reduce.4.cloned.1.call-start = ((), (), s32[]{:S(2)}) async-start(), calls=%async_computation.3 | async-start | bytes 1048576 | tf_op jit(solution)/shard_map/psum | solution.py:53
  386.5 284.1 %reduce-scatter.12.cloned.1.call-start = ((), (), s32[]{:S(2)}) async-start(), calls=%async_computation.10 | async-start | bytes 540672
  458.4 420.0 %all-reduce.6.cloned.1.call-start = ((), (), s32[]{:S(2)}) async-start(), calls=%async_computation.4 | async-start | bytes 1048576 | tf_op jit(solution)/shard_map/psum | solution.py:53
  809.9 284.2 %reduce-scatter.14.cloned.1.call-start = ((), (), s32[]{:S(2)}) async-start(), calls=%async_computation.11 | async-start | bytes 540672
  879.5 366.8 %copy-start.3 = (bf16[3,256,64]{1,2,0:T(8,128)(2,1)S(1)}, bf16[3,256,64]{1,2,0:T(8,128)(2,1)}, u32[]{:S(2)}) copy-start(bf16[3,256,64]{1,2,0:T(8,128)(2,1)} %param.14) | copy-start | bytes 294916
  881.9 362.6 %all-gather.7.cloned.1.call-start = ((), (), s32[]{:S(2)}) async-start(), calls=%async_computation.6 | async-start | bytes 2162688 | tf_op jit(solution)/shard_map/all_gather | solution.py:63
  884.4 516.8 %all-gather.9.cloned.1.call-start = ((), (), s32[]{:S(2)}) async-start(), calls=%async_computation.7 | async-start | bytes 2162688 | tf_op jit(solution)/shard_map/all_gather | solution.py:63
  1327.2 150.7 %all-reduce.8.cloned.1.call-start = ((), (), s32[]{:S(2)}) async-start(), calls=%async_computation.5 | async-start | bytes 1048576 | tf_op jit(solution)/shard_map/psum | solution.py:53
  1329.6 221.9 %all-gather.11.cloned.1.call-start = ((), (), s32[]{:S(2)}) async-start(), calls=%async_computation.8 | async-start | bytes 2162688 | tf_op jit(solution)/shard_map/all_gather | solution.py:63
  1479.7 146.1 %copy-start.1 = (f32[64,2048]{1,0:T(8,128)}, f32[64,2048]{1,0:T(8,128)S(1)}, u32[]{:S(2)}) copy-start(f32[64,2048]{1,0:T(8,128)S(1)} %select_dynamic-update-slice_fusion.3) | copy-start | bytes 1572868
  1625.8 0.8 copy-start
Sparse Core Ops, SparseCore 0:
  32.2 214.8 reduce-scatter.9
  386.6 68.2 all-reduce.3
  459.2 211.2 reduce-scatter.11
  810.0 68.2 all-reduce.5
  882.6 211.4 reduce-scatter.13
  1097.4 75.8 all-gather.6
  1327.3 73.8 all-gather.8
  1404.2 64.6 all-reduce.7
  1478.0 73.4 all-gather.10
